TPU v7x, 512 devices: a whole 4x4x16 slice. The times are simulated.
512 devices in a mesh: batch: 64 (over y, z), tensor: 8 (over x, core).
Axes of the slice: x: 4, y: 4, z: 16, core: 2. Of those that a mesh axis runs over, the one named last changes fastest.
Arguments:
- tokens: bfloat16 [8192, 8192], P('batch', 'tensor'), may hold values from -6 to 6
- cotangent: bfloat16 [8192, 8192], P('batch', 'tensor'), may hold values from -1.5 to 1.5
- game_ids: int32 [8192], P('batch'), may hold values from 0 to 31, as said below
- adapters: bfloat16 [64, 8192, 1024], P('batch', 'tensor'), may hold values from -0.1875 to 0.1875
Outputs:
- input_grad: bfloat16 [8192, 8192], P('batch', 'tensor')
- adapter_grad: bfloat16 [64, 8192, 1024], P('batch', 'tensor')
Inputs may be any that keep to these rules, and one draw needn't show every extreme that they name: `game_ids`: among the 128 tokens of each batch index no game appears more than 8 times; one game, the same for every batch index, appears exactly 8 times at every batch index.
All inputs are finite; a program needn't handle non-finite values.
Results may differ from a plain program's by a relative error of at most 0.0056.
Values may be sent and summed in bfloat16 or wider, within the bound.
A program may use at most 64 MiB of HBM per device.

v0:
```python
import jax
import jax.numpy as jnp
from jax import lax
from jax.sharding import PartitionSpec as P

GELU_SCALE = 0.7978845608028654
GELU_CUBIC = 0.044715


def partner_2(shard, axis, distance):
    return lax.ppermute(shard, axis, [(i, i ^ 1 << distance) for i in range(lax.axis_size(axis))])


def smooth_gate(values_in):
    inner_arg = GELU_SCALE * (values_in + GELU_CUBIC * values_in * values_in * values_in)
    return 0.5 * values_in * (1.0 + jnp.tanh(inner_arg))


def gate_slope(values_in):
    inner_arg = GELU_SCALE * (values_in + GELU_CUBIC * values_in * values_in * values_in)
    tangent = jnp.tanh(inner_arg)
    return 0.5 * (1.0 + tangent) + 0.5 * values_in * (1.0 - tangent * tangent) * GELU_SCALE * (
        1.0 + 3.0 * GELU_CUBIC * values_in * values_in
    )


def body(tokens, cotangent, game_ids, adapters):
    tok_rows, features = tokens.shape
    owner_count = lax.axis_size("batch")
    game_count = owner_count // 2
    slot_count = 2 * tok_rows // game_count
    received_rows = owner_count * slot_count
    leading = lax.axis_index("batch") % 2 == 0
    weight = adapters[0]
    columns = weight.shape[1]
    contract_rows = (((0,), (0,)), ((), ()))
    contract_cols = (((1,), (1,)), ((), ()))
    labels = jnp.arange(game_count, dtype=jnp.int32)
    member = (game_ids[:, None] == labels[None, :]).astype(jnp.int32)
    before = jnp.cumsum(member, axis=0) - member
    position = jnp.sum(before * member, axis=1)
    target = game_ids * slot_count + position
    places = jnp.arange(game_count * slot_count, dtype=jnp.int32)
    placing = (places[:, None] == target[None, :]).astype(jnp.bfloat16)
    sent_tokens = jnp.dot(placing, tokens, preferred_element_type=jnp.float32).astype(jnp.bfloat16)
    sent_grads = jnp.dot(placing, cotangent, preferred_element_type=jnp.float32).astype(
        jnp.bfloat16
    )
    outgoing = jnp.concatenate(
        [
            sent_tokens.reshape(game_count, 1, slot_count, features),
            sent_grads.reshape(game_count, 1, slot_count, features),
        ],
        axis=1,
    ).reshape(received_rows, features)
    arrived = lax.all_to_all(outgoing, "batch", split_axis=0, concat_axis=0, tiled=True)
    row_block = arrived
    summed = lax.psum_scatter(
        jnp.dot(row_block, weight, preferred_element_type=jnp.float32),
        "tensor",
        scatter_dimension=0,
        tiled=True,
    )
    sending = jnp.where(leading, smooth_gate(summed), summed).astype(jnp.bfloat16)
    partner = partner_2(sending, "batch", 0)
    partner_wide = partner.astype(jnp.float32)
    mixed_rows = jnp.where(leading, partner_wide * gate_slope(summed), partner_wide).astype(
        jnp.bfloat16
    )
    piece_rows = lax.all_gather(mixed_rows, "tensor", axis=0, tiled=True)
    row_block = arrived
    running = lax.dot_general(
        row_block, piece_rows, contract_rows, preferred_element_type=jnp.float32
    )
    rows_back = lax.cond(
        leading,
        lambda: lax.dot_general(
            piece_rows, weight, contract_cols, preferred_element_type=jnp.float32
        ).astype(jnp.bfloat16),
        lambda: jnp.zeros((piece_rows.shape[0], features), jnp.bfloat16),
    )
    arrived_back = lax.all_to_all(rows_back, "batch", split_axis=0, concat_axis=0, tiled=True)
    gathered = arrived_back.reshape(game_count, 2, slot_count, features)[:, 0].reshape(
        game_count * slot_count, features
    )
    result = lax.dot_general(
        placing, gathered, contract_rows, preferred_element_type=jnp.float32
    ).astype(jnp.bfloat16)
    return (result, running.astype(jnp.bfloat16).reshape(1, features, columns))


def solution(mesh):
    return jax.shard_map(
        body,
        mesh=mesh,
        in_specs=(
            P("batch", "tensor"),
            P("batch", "tensor"),
            P("batch"),
            P("batch", "tensor", None),
        ),
        out_specs=(P("batch", "tensor"), P("batch", "tensor", None)),
        check_vma=False,
    )
```

profile of v0, /device:TPU:1, one launch (start us, length us, event | category | flops | bytes accessed | tf_op | source)
XLA Modules:
  0.0 238.9 jit_solution(7873725473631197825)
XLA Ops:
  7.2 0.0 copy-start
  7.2 0.0 reduce-scatter.2.cloned.1.call-start
  7.2 0.8 fusion.14
  8.0 0.2 reduce_window_sum.11
  8.2 0.8 select_reduce_fusion
  9.0 0.7 multiply_add_fusion.1
  9.7 0.0 copy-done
  9.7 0.3 fusion.1
  10.0 1.2 fusion
  11.2 0.0 copy-start.1
  11.2 0.1 pad_maximum_fusion
  11.3 69.5 %all_to_all.21 = bf16[64,8,1024]{2,1,0:T(8,128)(2,1)S(1)} all-to-all(bf16[64,8,1024]{2,1,0:T(8,128)(2,1)S(1)} %bitcast.29), channel_id=1, replica_groups=mesh['batch'=64,'tensor'=8] {'batch'}, dimensions={0} | all-to-all | bytes 2097152 | tf_op jit(solution)/shard_map/all_to_all | solution.py:56
  80.9 0.0 copy-done.1
  80.9 2.6 %fusion.3 = f32[512,1024]{1,0:T(8,128)} fusion(bf16[64,8,1024]{2,1,0:T(8,128)(2,1)S(1)} %all_to_all.21, bf16[1,1024,1024]{2,1,0:T(8,128)(2,1)S(1)} %copy-done.1), kind=kOutput, calls=%fused_computation.9 | convolution fusion | flops 1073741824 | bytes 5242880 | tf_op jit(solution)/shard_map/dot_general | solution.py:59
  83.4 0.0 reduce-scatter.2.cloned.1.call-update
  83.5 0.0 all-gather.2.cloned.1.call-start
  83.5 35.9 %reduce-scatter.2.cloned.1.call-done = f32[64,1024]{1,0:T(8,128)} async-done(((f32[512,1024]{1,0:T(8,128)}), f32[64,1024]{1,0:T(8,128)}) %reduce-scatter.2.cloned.1.call-update) | async-done | bytes 262160 | tf_op jit(solution)/shard_map/reduce_scatter | solution.py:58
  119.4 1.0 select_convert_fusion
  120.5 2.2 collective-permute-start
  122.7 3.5 %collective-permute-done = bf16[64,1024]{1,0:T(8,128)(2,1)S(1)} collective-permute-done((bf16[64,1024]{1,0:T(8,128)(2,1)S(1)}, bf16[64,1024]{1,0:T(8,128)(2,1)S(1)}, u32[]{:S(2)}, u32[]{:S(2)}) %collective-permute-start) | collective-permute-done | bytes 131104 | tf_op jit(solution)/shard_map/ppermute | solution.py:11
  126.2 1.8 fusion.10
  128.0 0.0 all-gather.2.cloned.1.call-update
  128.0 33.7 %all-gather.2.cloned.1.call-done = bf16[512,1024]{1,0:T(8,128)(2,1)} async-done(((bf16[64,1024]{1,0:T(8,128)(2,1)}), bf16[512,1024]{1,0:T(8,128)(2,1)}) %all-gather.2.cloned.1.call-update) | async-done | bytes 1048592 | tf_op jit(solution)/shard_map/all_gather | solution.py:70
  161.7 3.5 %conditional.1 = (bf16[512,1024]{1,0:T(8,128)(2,1)}) conditional(s32[]{:T(128)} %convert_element_type.32, () %tuple.14, (bf16[512,1024]{1,0:T(8,128)(2,1)}, bf16[1024,1024]{1,0:T(8,128)(2,1)S(1)}) %tuple.23), branch_computations={%region_3.4_spmd, %region_4.5_spmd} | conditional | flops 1074266112 | bytes 4194312 | solution.py:75
  161.7 3.5 %convolution_convert_fusion = bf16[512,1024]{1,0:T(8,128)(2,1)} fusion(bf16[512,1024]{1,0:T(8,128)(2,1)} %get-tuple-element.4, bf16[1024,1024]{1,0:T(8,128)(2,1)S(1)} %get-tuple-element.8), kind=kOutput, calls=%fused_computation | convolution fusion | flops 1074266112 | bytes 4194304 | tf_op jit(solution)/shard_map/cond/branch_1_fun/dot_general | solution.py:77
  165.2 0.0 copy-start.2
  165.2 15.3 %all-to-all-start.1 = ((bf16[64,8,1024]{2,1,0:T(8,128)(2,1)}), bf16[64,8,1024]{2,1,0:T(8,128)(2,1)S(1)}, u32[]{:S(2)}, u32[]{:S(2)}) async-start(bf16[64,8,1024]{2,1,0:T(8,128)(2,1)} %bitcast.7), calls=%async_computation.2 | async-start | bytes 2097152 | tf_op jit(solution)/shard_map/all_to_all | solution.py:82
  180.6 0.0 copy-done.2
  180.6 2.6 %convert_bitcast_fusion = bf16[1,1024,1024]{2,1,0:T(8,128)(2,1)} fusion(bf16[512,1024]{1,0:T(8,128)(2,1)S(1)} %copy-done.2, bf16[64,8,1024]{2,1,0:T(8,128)(2,1)S(1)} %all_to_all.21), kind=kOutput, calls=%fused_computation.1 | convolution fusion | flops 1074790400 | bytes 4194304 | tf_op jit(solution)/shard_map/dot_general | solution.py:72
  183.2 47.9 %all-to-all-done.1 = bf16[64,8,1024]{2,1,0:T(8,128)(2,1)S(1)} async-done(((bf16[64,8,1024]{2,1,0:T(8,128)(2,1)}), bf16[64,8,1024]{2,1,0:T(8,128)(2,1)S(1)}, u32[]{:S(2)}, u32[]{:S(2)}) %all-to-all-start.1) | async-done | bytes 1048608 | tf_op jit(solution)/shard_map/all_to_all | solution.py:82
  231.1 1.0 convolution_convert_fusion.3
Async XLA Ops:
  7.2 2.5 %copy-start = (bf16[128,1024]{1,0:T(8,128)(2,1)S(1)}, bf16[128,1024]{1,0:T(8,128)(2,1)}, u32[]{:S(2)}) copy-start(bf16[128,1024]{1,0:T(8,128)(2,1)} %param.7) | copy-start | bytes 786436
  7.2 112.3 %reduce-scatter.2.cloned.1.call-start = ((), (), s32[]{:S(2)}) async-start(), calls=%async_computation.3 | async-start | bytes 2359296 | tf_op jit(solution)/shard_map/reduce_scatter | solution.py:58
  11.2 69.6 %copy-start.1 = (bf16[1,1024,1024]{2,1,0:T(8,128)(2,1)S(1)}, bf16[1,1024,1024]{2,1,0:T(8,128)(2,1)}, u32[]{:S(2)}) copy-start(bf16[1,1024,1024]{2,1,0:T(8,128)(2,1)} %param.9) | copy-start | bytes 6291460
  83.5 78.2 %all-gather.2.cloned.1.call-start = ((), (), s32[]{:S(2)}) async-start(), calls=%async_computation.4 | async-start | bytes 1179648 | tf_op jit(solution)/shard_map/all_gather | solution.py:70
  120.5 5.7 %collective-permute-start = (bf16[64,1024]{1,0:T(8,128)(2,1)S(1)}, bf16[64,1024]{1,0:T(8,128)(2,1)S(1)}, u32[]{:S(2)}, u32[]{:S(2)}) collective-permute-start(bf16[64,1024]{1,0:T(8,128)(2,1)S(1)} %select_convert_fusion), channel_id=1, source_target_pairs={{0,8},{8,0},{16,24},{24,16},{32,40},{40,32},{48,56},{56,48},{64,72... | collective-permute-start | bytes 393224 | tf_op jit(solution)/shard_map/ppermute | solution.py:11
  165.2 15.3 %copy-start.2 = (bf16[512,1024]{1,0:T(8,128)(2,1)S(1)}, bf16[512,1024]{1,0:T(8,128)(2,1)}, u32[]{:S(2)}) copy-start(bf16[512,1024]{1,0:T(8,128)(2,1)} %all-gather.2.cloned.1.call-done) | copy-start | bytes 3145732
  165.2 65.9 %all-to-all-start.1 = ((bf16[64,8,1024]{2,1,0:T(8,128)(2,1)}), bf16[64,8,1024]{2,1,0:T(8,128)(2,1)S(1)}, u32[]{:S(2)}, u32[]{:S(2)}) async-start(bf16[64,8,1024]{2,1,0:T(8,128)(2,1)} %bitcast.7), calls=%async_computation.2 | async-start | bytes 2097152 | tf_op jit(solution)/shard_map/all_to_all | solution.py:82
Sparse Core Ops, SparseCore 0:
  83.6 35.8 reduce-scatter.1
  128.1 33.4 all-gather.1
where the time goes:
time: 242 us; the launch traced here: 239 us
  waiting for transfers between devices  121 us (50%)
  blocking collectives  69.5 us (29%)
  starting transfers between devices  17.6 us (7%)
  between operations  14.1 us (6%)
  matrix products  11.2 us (5%)
  other arithmetic  5.37 us (2%)
    all_to_all x1, blocking collectives, body(): lax.all_to_all(outgoing, 'batch', split_axis=0, concat_axis=0, tiled=True)  69.5 us
    all_to_all x1, waiting for transfers between devices, body(): lax.all_to_all(rows_back, 'batch', split_axis=0, concat_axis=0, tiled=True)  47.9 us
    reduce_scatter x1, waiting for transfers between devices, body(): lax.psum_scatter(jnp.dot(row_block, weight, preferred_element_type=jnp.fl...  35.9 us
    all_gather x1, waiting for transfers between devices, body(): piece_rows = lax.all_gather(mixed_rows, 'tensor', axis=0, tiled=True)  33.7 us
    all_to_all x1, starting transfers between devices, body(): lax.all_to_all(rows_back, 'batch', split_axis=0, concat_axis=0, tiled=True)  15.3 us
  transfers between devices with their start and end apart: 4, of which 4 were waited for; matrix products, arithmetic and copies ran while one was open for 1% of the time, Pallas kernels for 0%

commit v1 on v0

v1 whole, which is shorter than its diff:
```python
import functools

import jax
import jax.numpy as jnp
from jax import lax
from jax.experimental import pallas as pl
from jax.experimental.pallas import tpu as pltpu
from jax.sharding import PartitionSpec as P

MESH = pl.DeviceIdType.MESH
GELU_SCALE = 0.7978845608028654
GELU_CUBIC = 0.044715
CAP = 8
NY = 4
F32 = jnp.float32
BF16 = jnp.bfloat16


def smooth_gate(v):
    inner = GELU_SCALE * (v + GELU_CUBIC * v * v * v)
    return 0.5 * v * (1.0 + jnp.tanh(inner))


def gate_slope(v):
    inner = GELU_SCALE * (v + GELU_CUBIC * v * v * v)
    tangent = jnp.tanh(inner)
    return 0.5 * (1.0 + tangent) + 0.5 * v * (1.0 - tangent * tangent) * GELU_SCALE * (
        1.0 + 3.0 * GELU_CUBIC * v * v
    )


def kernel(
    ny, nz, nt, part_type,
    ids_ref, tok_hbm, cot_hbm, w_hbm,
    ig_hbm, ag_hbm,
    tok, cot, w, sends, arrived, rows, part, summands, swap_out, swap_in, mixed, bsend, back, ig, ag,
    in_sem, out_sem, self_sem, fwd_send, fwd_recv, rs_send, rs_recv, swap_send, swap_recv, ag_send, ag_recv,
    back_send, back_recv,
):
    nb = ny * nz
    np_ = nz // 2
    me = lax.axis_index("batch")
    t = lax.axis_index("tensor")
    y, z = me // nz, me % nz
    p, par = z // 2, z % 2
    count, features = tok.shape
    hidden = w.shape[1]
    half = features // 2
    games = nb // 2
    chunk = nz * CAP
    piece = chunk // nt

    copies = [
        pltpu.make_async_copy(a, b, in_sem.at[i])
        for i, (a, b) in enumerate(((tok_hbm, tok), (cot_hbm, cot), (w_hbm, w)))
    ]
    for c in copies:
        c.start()

    barrier = pltpu.get_barrier_semaphore()

    def greet_batch(k, _):
        pl.semaphore_signal(barrier, inc=1, device_id={"batch": (me + k) % nb}, device_id_type=MESH)
        return _

    def greet_tensor(k, _):
        pl.semaphore_signal(barrier, inc=1, device_id={"tensor": (t + k) % nt}, device_id_type=MESH)
        return _

    lax.fori_loop(1, nb, greet_batch, 0)
    lax.fori_loop(1, nt, greet_tensor, 0)

    ids = ids_ref[...]
    member = (lax.broadcasted_iota(jnp.int32, (games, count), 0) == ids).astype(F32)
    earlier = (
        lax.broadcasted_iota(jnp.int32, (count, count), 0) < lax.broadcasted_iota(jnp.int32, (count, count), 1)
    ).astype(F32)
    before = jnp.dot(member.astype(BF16), earlier.astype(BF16), preferred_element_type=F32)
    position = jnp.sum(before * member, axis=0, keepdims=True).astype(jnp.int32)
    gy, gp = ids // np_, ids % np_
    target = (((gy - y + ny) % ny) * np_ + (gp - p + np_) % np_) * CAP + position

    place = lax.broadcasted_iota(jnp.int32, (2 * games * CAP, count), 0)
    slot = (place // 16) * CAP + place % CAP
    placing = (slot == target).astype(BF16)
    on_left = lax.broadcasted_iota(jnp.int32, (2 * games * CAP, half), 0) % 16 < 8
    for q in range(2):
        copies[q].wait()
        src = (tok, cot)[q]
        left = jnp.dot(placing, src[:, :half], preferred_element_type=F32)
        right = jnp.dot(placing, src[:, half:], preferred_element_type=F32)
        sends[q] = jnp.where(on_left, left, right).astype(BF16).reshape(games, 16, half)

    pl.semaphore_wait(barrier, nb - 1 + nt - 1)

    own_block = pltpu.make_async_copy(sends.at[par, 0], arrived.at[0, par], self_sem.at[0])
    own_block.start()

    def send_forward(j, _):
        dy, r = j // np_, j % np_
        dp = (np_ // 2 + (r % 2) * (r + 1) // 2 - ((r + 1) % 2) * (r // 2) + np_) % np_
        far_y = (y + dy) % ny
        far_p = (p + dp) % np_
        for q in range(2):
            far = far_y * nz + 2 * far_p + q

            @pl.when(far != me)
            def _send():
                pltpu.make_async_remote_copy(
                    src_ref=sends.at[q, dy * np_ + dp],
                    dst_ref=arrived.at[dy, 2 * dp + par],
                    send_sem=fwd_send,
                    recv_sem=fwd_recv.at[dy],
                    device_id={"batch": far},
                    device_id_type=MESH,
                ).start()

        return _

    lax.fori_loop(0, ny * np_, send_forward, 0)
    copies[2].wait()

    tile = min(256, hidden)

    def per_chunk(c, _):
        @pl.when(c == 0)
        def _first():
            own_block.wait()
            ref = arrived.at[0, pl.ds(0, nz - 1)]
            pltpu.make_async_copy(ref, ref, fwd_recv.at[0]).wait()

        @pl.when(c != 0)
        def _later():
            ref = arrived.at[c]
            pltpu.make_async_copy(ref, ref, fwd_recv.at[c]).wait()

        wide = arrived[c].astype(F32).reshape(nz, 2, CAP, half)
        rows[c, :, :half] = wide[:, 0].reshape(chunk, half).astype(BF16)
        rows[c, :, half:] = wide[:, 1].reshape(chunk, half).astype(BF16)

        def times_w(j, _):
            cols = pl.ds(pl.multiple_of(j * tile, tile), tile)
            product = jnp.dot(rows[c], w[:, cols], preferred_element_type=F32)
            part[c, :, :, cols] = product.reshape(nt, piece, tile).astype(part_type)
            return _

        lax.fori_loop(0, hidden // tile, times_w, 0)

        def send_part(k, _):
            far = (t + k) % nt
            pltpu.make_async_remote_copy(
                src_ref=part.at[c, far],
                dst_ref=summands.at[c, k - 1],
                send_sem=rs_send,
                recv_sem=rs_recv.at[c],
                device_id={"tensor": far},
                device_id_type=MESH,
            ).start()
            return _

        lax.fori_loop(1, nt, send_part, 0)
        ref = summands.at[c]
        pltpu.make_async_copy(ref, ref, rs_recv.at[c]).wait()
        total = part[c, t].astype(F32)
        for k in range(nt - 1):
            total = total + summands[c, k].astype(F32)
        swap_out[c] = jnp.where(par == 0, smooth_gate(total), total).astype(BF16)
        swap = pltpu.make_async_remote_copy(
            src_ref=swap_out.at[c],
            dst_ref=swap_in.at[c],
            send_sem=swap_send,
            recv_sem=swap_recv.at[c],
            device_id={"batch": me + 1 - 2 * par},
            device_id_type=MESH,
        )
        swap.start()
        slope = jnp.where(par == 0, gate_slope(total), 1.0)
        swap.wait_recv()
        mixed[c, t] = (swap_in[c].astype(F32) * slope).astype(BF16)

        def send_mixed(k, _):
            pltpu.make_async_remote_copy(
                src_ref=mixed.at[c, t],
                dst_ref=mixed.at[c, t],
                send_sem=ag_send,
                recv_sem=ag_recv.at[c],
                device_id={"tensor": (t + k) % nt},
                device_id_type=MESH,
            ).start()
            return _

        lax.fori_loop(1, nt, send_mixed, 0)
        ref = mixed.at[c, pl.ds(0, nt - 1)]
        pltpu.make_async_copy(ref, ref, ag_recv.at[c]).wait()

        @pl.when(par == 0)
        def _input_gradient():
            grad = lax.dot_general(
                mixed[c].reshape(chunk, hidden), w[...], (((1,), (1,)), ((), ())), preferred_element_type=F32
            )
            pair = jnp.stack(
                [grad[:, :half].reshape(nz, CAP, half), grad[:, half:].reshape(nz, CAP, half)], axis=1
            )
            bsend[c] = pair.reshape(nz, 16, half).astype(BF16)

            def send_back(j, _):
                dp, from_par = j // 2, j % 2
                far = ((y - c + ny) % ny) * nz + 2 * ((p - dp + np_) % np_) + from_par

                @pl.when(far != me)
                def _send():
                    pltpu.make_async_remote_copy(
                        src_ref=bsend.at[c, j],
                        dst_ref=back.at[c * np_ + dp],
                        send_sem=back_send,
                        recv_sem=back_recv,
                        device_id={"batch": far},
                        device_id_type=MESH,
                    ).start()

                @pl.when(far == me)
                def _keep():
                    pltpu.make_async_copy(bsend.at[0, 0], back.at[0], self_sem.at[1]).start()

                return _

            lax.fori_loop(0, nz, send_back, 0)

        return _

    lax.fori_loop(0, ny, per_chunk, 0)

    every = ny * chunk

    def adapter_columns(j, _):
        cols = pl.ds(pl.multiple_of(j * tile, tile), tile)
        product = lax.dot_general(
            rows[...].reshape(every, features), mixed[:, :, :, cols].reshape(every, tile), (((0,), (0,)), ((), ())),
            preferred_element_type=F32,
        )
        ag[:, cols] = product.astype(BF16)
        return _

    lax.fori_loop(0, hidden // tile, adapter_columns, 0)
    ag_copy = pltpu.make_async_copy(ag, ag_hbm, out_sem.at[0])
    ag_copy.start()

    eye = lax.broadcasted_iota(jnp.int32, (count, count), 0) == lax.broadcasted_iota(jnp.int32, (count, count), 1)
    target_column = jnp.sum(jnp.where(eye, target, 0), axis=1, keepdims=True)
    taking = (lax.broadcasted_iota(jnp.int32, (count, games * CAP), 1) == target_column).astype(BF16)

    @pl.when(par == 0)
    def _with_own():
        pltpu.make_async_copy(bsend.at[0, 0], back.at[0], self_sem.at[1]).wait()
        ref = back.at[pl.ds(0, games - 1)]
        pltpu.make_async_copy(ref, ref, back_recv).wait()

    @pl.when(par != 0)
    def _without_own():
        pltpu.make_async_copy(back, back, back_recv).wait()

    wide = back[...].astype(F32).reshape(games, 2, CAP, half)
    for h in range(2):
        side = wide[:, h].reshape(games * CAP, half).astype(BF16)
        ig[:, h * half:(h + 1) * half] = jnp.dot(taking, side, preferred_element_type=F32).astype(BF16)
    ig_copy = pltpu.make_async_copy(ig, ig_hbm, out_sem.at[1])
    ig_copy.start()

    ref = sends.at[:, pl.ds(0, games - 1)]
    pltpu.make_async_copy(ref, ref, fwd_send).wait()
    ref = sends.at[0, 0]
    pltpu.make_async_copy(ref, ref, fwd_send).wait()
    ref = summands
    pltpu.make_async_copy(ref, ref, rs_send).wait()
    pltpu.make_async_copy(swap_out, swap_out, swap_send).wait()
    ref = mixed.at[:, pl.ds(0, nt - 1)]
    pltpu.make_async_copy(ref, ref, ag_send).wait()

    @pl.when(par == 0)
    def _sent_back():
        for ref in (bsend.at[pl.ds(0, ny - 1)], bsend.at[0, pl.ds(0, nz - 1)]):
            pltpu.make_async_copy(ref, ref, back_send).wait()

    ag_copy.wait()
    ig_copy.wait()


def solution(mesh, ny=NY, part_type=BF16, interpret=False):
    nb, nt = mesh.shape["batch"], mesh.shape["tensor"]
    nz = nb // ny

    def body(tokens, cotangent, game_ids, adapters):
        count, features = tokens.shape
        hidden = adapters.shape[2]
        games = nb // 2
        half = features // 2
        chunk = nz * CAP
        piece = chunk // nt
        dma = pltpu.SemaphoreType.DMA
        any_ = pl.BlockSpec(memory_space=pl.ANY)
        ig, ag = pl.pallas_call(
            functools.partial(kernel, ny, nz, nt, part_type),
            out_shape=(
                jax.ShapeDtypeStruct((count, features), BF16),
                jax.ShapeDtypeStruct((features, hidden), BF16),
            ),
            in_specs=[pl.BlockSpec(memory_space=pltpu.VMEM), any_, any_, any_],
            out_specs=(any_, any_),
            scratch_shapes=[
                pltpu.VMEM((count, features), BF16),
                pltpu.VMEM((count, features), BF16),
                pltpu.VMEM((features, hidden), BF16),
                pltpu.VMEM((2, games, 16, half), BF16),
                pltpu.VMEM((ny, nz, 16, half), BF16),
                pltpu.VMEM((ny, chunk, features), BF16),
                pltpu.VMEM((ny, nt, piece, hidden), part_type),
                pltpu.VMEM((ny, nt - 1, piece, hidden), part_type),
                pltpu.VMEM((ny, piece, hidden), BF16),
                pltpu.VMEM((ny, piece, hidden), BF16),
                pltpu.VMEM((ny, nt, piece, hidden), BF16),
                pltpu.VMEM((ny, nz, 16, half), BF16),
                pltpu.VMEM((games, 16, half), BF16),
                pltpu.VMEM((count, features), BF16),
                pltpu.VMEM((features, hidden), BF16),
                dma((3,)), dma((2,)), dma((2,)),
                dma, dma((ny,)),
                dma, dma((ny,)),
                dma, dma((ny,)),
                dma, dma((ny,)),
                dma, dma,
            ],
            compiler_params=pltpu.CompilerParams(
                collective_id=0, has_side_effects=True, vmem_limit_bytes=48 << 20
            ),
            interpret=interpret,
        )(game_ids.reshape(1, count), tokens, cotangent, adapters.reshape(features, hidden))
        return ig, ag.reshape(1, features, hidden)

    return jax.shard_map(
        body,
        mesh=mesh,
        in_specs=(P("batch", "tensor"), P("batch", "tensor"), P("batch"), P("batch", "tensor", None)),
        out_specs=(P("batch", "tensor"), P("batch", "tensor", None)),
        check_vma=False,
    )
```

time: 242 us -> 134 us (0.55); the launches traced: 239 us -> 134 us
  Pallas kernels: 0 us -> 127 us
  waiting for transfers between devices: 121 us -> 0 us
  blocking collectives: 69.5 us -> 0 us
  starting transfers between devices: 17.6 us -> 0 us
  between operations: 14.1 us -> 0.65 us
  matrix products: 11.2 us -> 0 us
  local copies, waits for them, and re-layouts: 0.02 us -> 6.16 us
  other arithmetic: 5.37 us -> 0 us
    pallas_call x0 -> x1, Pallas kernels: none -> 127 us  [body(): pl.pallas_call(functools.partial(kernel, ny, nz, nt, part_type), out_shap...]
    all_to_all x1 -> x0, blocking collectives: 69.5 us -> none  [body(): lax.all_to_all(outgoing, 'batch', split_axis=0, concat_axis=0, tiled=True)]
    all_to_all x1 -> x0, waiting for transfers between devices: 47.9 us -> none  [body(): lax.all_to_all(rows_back, 'batch', split_axis=0, concat_axis=0, tiled=True)]
    reduce_scatter x1 -> x0, waiting for transfers between devices: 35.9 us -> none  [body(): lax.psum_scatter(jnp.dot(row_block, weight, preferred_element_type=jnp.fl...]
    all_gather x1 -> x0, waiting for transfers between devices: 33.7 us -> none  [body(): piece_rows = lax.all_gather(mixed_rows, 'tensor', axis=0, tiled=True)]
    all_to_all x1 -> x0, starting transfers between devices: 15.3 us -> none  [body(): lax.all_to_all(rows_back, 'batch', split_axis=0, concat_axis=0, tiled=True)]
    dot_general x6 -> x0, matrix products: 11.2 us -> none  [the longest x1 3.55 us: body(): lax.dot_general(piece_rows, weight, contract_cols, preferred_element_type...]
    unnamed x6 -> x10, local copies, waits for them, and re-layouts: 0.02 us -> 6.16 us
  transfers between devices with their start and end apart: 4 -> 0, of which waited for: 4 -> 0; matrix products, arithmetic and copies ran while one was open for 1% -> 0% of each run, Pallas kernels for 0% -> 0%
where the time goes in v1:
time: 134 us
  Pallas kernels  127 us (95%)
  local copies, waits for them, and re-layouts  6.16 us (5%)
    pallas_call x1, Pallas kernels, body(): pl.pallas_call(functools.partial(kernel, ny, nz, nt, part_type), out_shap...  127 us
    unnamed x10, local copies, waits for them, and re-layouts  6.16 us

profile of v1, /device:TPU:1, one launch (start us, length us, event | category | flops | bytes accessed | tf_op | source)
XLA Modules:
  0.0 133.7 jit_solution(1022199968531468445)
XLA Ops:
  0.6 0.0 copy-start
  0.6 1.6 %copy-done = bf16[1,1024,1024]{2,1,0:T(8,128)(2,1)S(1)} copy-done((bf16[1,1024,1024]{2,1,0:T(8,128)(2,1)S(1)}, bf16[1,1024,1024]{2,1,0:T(8,128)(2,1)}, u32[]{:S(2)}) %copy-start) | copy-done | bytes 2097176
  2.2 0.0 copy-start.1
  2.2 0.9 copy-done.1
  3.2 0.0 copy-start.2
  3.2 0.9 copy-done.2
  4.1 0.0 copy-start.3
  4.1 0.7 copy-done.3
  4.8 126.9 %shard_map.59 = (bf16[128,1024]{1,0:T(8,128)(2,1)S(1)}, bf16[1024,1024]{1,0:T(8,128)(2,1)S(1)}) custom-call(s32[1,128]{1,0:T(1,128)S(1)} %bitcast.5, bf16[128,1024]{1,0:T(8,128)(2,1)S(1)} %copy-done.1, bf16[128,1024]{1,0:T(8,128)(2,1)S(1)} %copy-done.2, bf16[1024,1024]{1,0:T(8,128)(2,1)S(1)} %bitcast.3), custom_call_target="tpu_custom_call" | custom-call | tf_op jit(solution)/shard_map/pallas_call | solution.py:301
  131.7 0.7 copy.8
  132.4 1.3 copy.9
Async XLA Ops:
  0.6 1.6 %copy-start = (bf16[1,1024,1024]{2,1,0:T(8,128)(2,1)S(1)}, bf16[1,1024,1024]{2,1,0:T(8,128)(2,1)}, u32[]{:S(2)}) copy-start(bf16[1,1024,1024]{2,1,0:T(8,128)(2,1)} %param.7) | copy-start | bytes 6291460
  2.2 0.9 copy-start.1
  3.2 0.9 copy-start.2
  4.1 0.7 copy-start.3

commit v2 on v1

--- a/solution.py
+++ b/solution.py
@@ -11,6 +11,7 @@
 GELU_SCALE = 0.7978845608028654
 GELU_CUBIC = 0.044715
 CAP = 8
+AHEAD = 2
 NY = 4
 F32 = jnp.float32
 BF16 = jnp.bfloat16
@@ -33,8 +34,8 @@
     ny, nz, nt, part_type,
     ids_ref, tok_hbm, cot_hbm, w_hbm,
     ig_hbm, ag_hbm,
-    tok, cot, w, sends, arrived, rows, part, summands, swap_out, swap_in, mixed, bsend, back, ig, ag,
-    in_sem, out_sem, self_sem, fwd_send, fwd_recv, rs_send, rs_recv, swap_send, swap_recv, ag_send, ag_recv,
+    tok, cot, w, sends, relay, arrived, rows, part, summands, swap_out, swap_in, slope, mixed, bsend, back, ig, ag,
+    in_sem, out_sem, self_sem, relay_send, relay_recv, fwd_send, fwd_recv, rs_send, rs_recv, swap_send, swap_recv, ag_send, ag_recv,
     back_send, back_recv,
 ):
     nb = ny * nz
@@ -43,12 +44,18 @@
     t = lax.axis_index("tensor")
     y, z = me // nz, me % nz
     p, par = z // 2, z % 2
+    core, x = t % 2, t // 2
+    sibling = t + 1 - 2 * core
+    gather_core = 1 - par
+    gathers = core == gather_core
     count, features = tok.shape
     hidden = w.shape[1]
     half = features // 2
     games = nb // 2
     chunk = nz * CAP
-    piece = chunk // nt
+    pieces = nt // 2
+    piece = chunk // pieces
+    up = np_ // 2
 
     copies = [
         pltpu.make_async_copy(a, b, in_sem.at[i])
@@ -89,40 +96,82 @@
         src = (tok, cot)[q]
         left = jnp.dot(placing, src[:, :half], preferred_element_type=F32)
         right = jnp.dot(placing, src[:, half:], preferred_element_type=F32)
-        sends[q] = jnp.where(on_left, left, right).astype(BF16).reshape(games, 16, half)
+        sends[:, q] = jnp.where(on_left, left, right).astype(BF16).reshape(games, 16, half)
 
     pl.semaphore_wait(barrier, nb - 1 + nt - 1)
 
-    own_block = pltpu.make_async_copy(sends.at[par, 0], arrived.at[0, par], self_sem.at[0])
+    own_block = pltpu.make_async_copy(sends.at[0, par], arrived.at[0, par], self_sem.at[0])
     own_block.start()
 
-    def send_forward(j, _):
-        dy, r = j // np_, j % np_
-        dp = (np_ // 2 + (r % 2) * (r + 1) // 2 - ((r + 1) % 2) * (r // 2) + np_) % np_
-        far_y = (y + dy) % ny
-        far_p = (p + dp) % np_
-        for q in range(2):
-            far = far_y * nz + 2 * far_p + q
-
-            @pl.when(far != me)
-            def _send():
+    def relay_part(dy, for_core):
+        first, number = ((1, up), (up + 1, up - 1))[for_core]
+        return sends.at[pl.ds(dy * np_ + first, number)], relay.at[dy, pl.ds(0, number)]
+
+    for c in range(2):
+
+        @pl.when(core != c)
+        def _hand_over():
+            def hand_over(dy, _):
+                src, dst = relay_part(dy, c)
                 pltpu.make_async_remote_copy(
-                    src_ref=sends.at[q, dy * np_ + dp],
-                    dst_ref=arrived.at[dy, 2 * dp + par],
-                    send_sem=fwd_send,
-                    recv_sem=fwd_recv.at[dy],
-                    device_id={"batch": far},
+                    src_ref=src,
+                    dst_ref=dst,
+                    send_sem=relay_send,
+                    recv_sem=relay_recv.at[dy],
+                    device_id={"tensor": sibling},
                     device_id_type=MESH,
                 ).start()
+                return _
+
+            lax.fori_loop(0, ny, hand_over, 0)
+
+    def send_block(src, dy, dp, q, tensor):
+        far = ((y + dy) % ny) * nz + 2 * ((p + dp) % np_) + q
+        pltpu.make_async_remote_copy(
+            src_ref=src,
+            dst_ref=arrived.at[dy, 2 * dp + par],
+            send_sem=fwd_send,
+            recv_sem=fwd_recv.at[dy],
+            device_id={"batch": far, "tensor": tensor},
+            device_id_type=MESH,
+        ).start()
+
+    def send_forward(dy, _):
+        for c in range(2):
+
+            @pl.when(core == c)
+            def _own_way():
+                number = up - c
+
+                def own(i, _):
+                    dp = up + 1 + i if c else up - i
+                    for q in range(2):
+                        send_block(sends.at[dy * np_ + dp, q], dy, dp, q, t)
+                    return _
+
+                def relayed(i, _):
+                    dp = up + 1 + i if c else up - i
+                    for q in range(2):
+                        send_block(relay.at[dy, i if c else up - 1 - i, q], dy, dp, q, sibling)
+                    return _
+
+                lax.fori_loop(0, number, own, 0)
+                _, ref = relay_part(dy, c)
+                pltpu.make_async_copy(ref, ref, relay_recv.at[dy]).wait()
+                lax.fori_loop(0, number, relayed, 0)
+
+        send_block(sends.at[dy * np_, 1 - par], dy, 0, 1 - par, t)
+
+        @pl.when(dy != 0)
+        def _straight():
+            send_block(sends.at[dy * np_, par], dy, 0, par, t)
 
         return _
 
-    lax.fori_loop(0, ny * np_, send_forward, 0)
+    lax.fori_loop(0, AHEAD, send_forward, 0)
     copies[2].wait()
 
-    tile = min(256, hidden)
-
-    def per_chunk(c, _):
+    def arrive(c):
         @pl.when(c == 0)
         def _first():
             own_block.wait()
@@ -134,54 +183,64 @@
             ref = arrived.at[c]
             pltpu.make_async_copy(ref, ref, fwd_recv.at[c]).wait()
 
+        @pl.when(c + AHEAD < ny)
+        def _next():
+            send_forward(c + AHEAD, 0)
+
         wide = arrived[c].astype(F32).reshape(nz, 2, CAP, half)
         rows[c, :, :half] = wide[:, 0].reshape(chunk, half).astype(BF16)
         rows[c, :, half:] = wide[:, 1].reshape(chunk, half).astype(BF16)
 
-        def times_w(j, _):
-            cols = pl.ds(pl.multiple_of(j * tile, tile), tile)
-            product = jnp.dot(rows[c], w[:, cols], preferred_element_type=F32)
-            part[c, :, :, cols] = product.reshape(nt, piece, tile).astype(part_type)
+        product = jnp.dot(rows[c], w[...], preferred_element_type=F32)
+        part[c] = product.reshape(pieces, piece, hidden).astype(part_type)
+
+        def send_part(k, _):
+            to = (x + k) % pieces
+
+            @pl.when(2 * to + gather_core != t)
+            def _send():
+                far = 2 * to + gather_core
+                pltpu.make_async_remote_copy(
+                    src_ref=part.at[c, to],
+                    dst_ref=summands.at[c, (t - far + nt) % nt - 1],
+                    send_sem=rs_send,
+                    recv_sem=rs_recv.at[c],
+                    device_id={"tensor": far},
+                    device_id_type=MESH,
+                ).start()
+
             return _
 
-        lax.fori_loop(0, hidden // tile, times_w, 0)
-
-        def send_part(k, _):
-            far = (t + k) % nt
-            pltpu.make_async_remote_copy(
-                src_ref=part.at[c, far],
-                dst_ref=summands.at[c, k - 1],
-                send_sem=rs_send,
-                recv_sem=rs_recv.at[c],
-                device_id={"tensor": far},
-                device_id_type=MESH,
-            ).start()
-            return _
-
-        lax.fori_loop(1, nt, send_part, 0)
-        ref = summands.at[c]
-        pltpu.make_async_copy(ref, ref, rs_recv.at[c]).wait()
-        total = part[c, t].astype(F32)
-        for k in range(nt - 1):
-            total = total + summands[c, k].astype(F32)
-        swap_out[c] = jnp.where(par == 0, smooth_gate(total), total).astype(BF16)
-        swap = pltpu.make_async_remote_copy(
+        lax.fori_loop(0, pieces, send_part, 0)
+
+    def swap_copy(c):
+        return pltpu.make_async_remote_copy(
             src_ref=swap_out.at[c],
             dst_ref=swap_in.at[c],
             send_sem=swap_send,
             recv_sem=swap_recv.at[c],
-            device_id={"batch": me + 1 - 2 * par},
+            device_id={"batch": me + 1 - 2 * par, "tensor": 2 * x + par},
             device_id_type=MESH,
         )
-        swap.start()
-        slope = jnp.where(par == 0, gate_slope(total), 1.0)
-        swap.wait_recv()
-        mixed[c, t] = (swap_in[c].astype(F32) * slope).astype(BF16)
+
+    def combine(c):
+        ref = summands.at[c]
+        pltpu.make_async_copy(ref, ref, rs_recv.at[c]).wait()
+        total = part[c, x].astype(F32)
+        for k in range(nt - 1):
+            total = total + summands[c, k].astype(F32)
+        swap_out[c] = jnp.where(par == 0, smooth_gate(total), total).astype(BF16)
+        swap_copy(c).start()
+        slope[...] = jnp.where(par == 0, gate_slope(total), 1.0)
+
+    def spread(c):
+        swap_copy(c).wait_recv()
+        mixed[c, x] = (swap_in[c].astype(F32) * slope[...]).astype(BF16)
 
         def send_mixed(k, _):
             pltpu.make_async_remote_copy(
-                src_ref=mixed.at[c, t],
-                dst_ref=mixed.at[c, t],
+                src_ref=mixed.at[c, x],
+                dst_ref=mixed.at[c, x],
                 send_sem=ag_send,
                 recv_sem=ag_recv.at[c],
                 device_id={"tensor": (t + k) % nt},
@@ -190,8 +249,15 @@
             return _
 
         lax.fori_loop(1, nt, send_mixed, 0)
-        ref = mixed.at[c, pl.ds(0, nt - 1)]
-        pltpu.make_async_copy(ref, ref, ag_recv.at[c]).wait()
+
+    def give_back(c):
+        for number, yes in ((pieces - 1, gathers), (pieces, jnp.logical_not(gathers))):
+            if number > 0:
+
+                @pl.when(yes)
+                def _wait():
+                    ref = mixed.at[c, pl.ds(0, number)]
+                    pltpu.make_async_copy(ref, ref, ag_recv.at[c]).wait()
 
         @pl.when(par == 0)
         def _input_gradient():
@@ -203,6 +269,9 @@
             )
             bsend[c] = pair.reshape(nz, 16, half).astype(BF16)
 
+    def start_back(c):
+        @pl.when(par == 0)
+        def _start():
             def send_back(j, _):
                 dp, from_par = j // 2, j % 2
                 far = ((y - c + ny) % ny) * nz + 2 * ((p - dp + np_) % np_) + from_par
@@ -226,22 +295,38 @@
 
             lax.fori_loop(0, nz, send_back, 0)
 
+    def per_chunk(k, _):
+        @pl.when(k < ny)
+        def _arrive():
+            arrive(k)
+
+        @pl.when(k > 0)
+        def _give_back():
+            give_back(k - 1)
+
+        @pl.when((k < ny) & gathers)
+        def _combine():
+            combine(k)
+
+        @pl.when(k > 0)
+        def _start_back():
+            start_back(k - 1)
+
+        @pl.when((k < ny) & gathers)
+        def _spread():
+            spread(k)
+
         return _
 
-    lax.fori_loop(0, ny, per_chunk, 0)
+    lax.fori_loop(0, ny + 1, per_chunk, 0)
 
     every = ny * chunk
 
-    def adapter_columns(j, _):
-        cols = pl.ds(pl.multiple_of(j * tile, tile), tile)
-        product = lax.dot_general(
-            rows[...].reshape(every, features), mixed[:, :, :, cols].reshape(every, tile), (((0,), (0,)), ((), ())),
-            preferred_element_type=F32,
-        )
-        ag[:, cols] = product.astype(BF16)
-        return _
-
-    lax.fori_loop(0, hidden // tile, adapter_columns, 0)
+    product = lax.dot_general(
+        rows[...].reshape(every, features), mixed[...].reshape(every, hidden), (((0,), (0,)), ((), ())),
+        preferred_element_type=F32,
+    )
+    ag[...] = product.astype(BF16)
     ag_copy = pltpu.make_async_copy(ag, ag_hbm, out_sem.at[0])
     ag_copy.start()
 
@@ -266,15 +351,33 @@
     ig_copy = pltpu.make_async_copy(ig, ig_hbm, out_sem.at[1])
     ig_copy.start()
 
-    ref = sends.at[:, pl.ds(0, games - 1)]
+    for c in range(2):
+
+        @pl.when(core == c)
+        def _sent():
+            for ref, sem in (
+                (relay.at[:, pl.ds(0, up - 1 + c)], relay_send),
+                (relay.at[:, pl.ds(0, up - c)], fwd_send),
+                (relay.at[:, pl.ds(0, up - c)], fwd_send),
+            ):
+                pltpu.make_async_copy(ref, ref, sem).wait()
+
+    ref = bsend.at[0, pl.ds(0, 2 * ny - 1)]
     pltpu.make_async_copy(ref, ref, fwd_send).wait()
-    ref = sends.at[0, 0]
-    pltpu.make_async_copy(ref, ref, fwd_send).wait()
-    ref = summands
-    pltpu.make_async_copy(ref, ref, rs_send).wait()
-    pltpu.make_async_copy(swap_out, swap_out, swap_send).wait()
-    ref = mixed.at[:, pl.ds(0, nt - 1)]
-    pltpu.make_async_copy(ref, ref, ag_send).wait()
+
+    @pl.when(gathers)
+    def _gathered():
+        if pieces > 1:
+            ref = part.at[:, pl.ds(0, pieces - 1)]
+            pltpu.make_async_copy(ref, ref, rs_send).wait()
+            ref = mixed.at[:, pl.ds(0, pieces - 1)]
+            pltpu.make_async_copy(ref, ref, ag_send).wait()
+        pltpu.make_async_copy(swap_out, swap_out, swap_send).wait()
+        pltpu.make_async_copy(mixed, mixed, ag_send).wait()
+
+    @pl.when(jnp.logical_not(gathers))
+    def _given():
+        pltpu.make_async_copy(part, part, rs_send).wait()
 
     @pl.when(par == 0)
     def _sent_back():
@@ -294,8 +397,10 @@
         hidden = adapters.shape[2]
         games = nb // 2
         half = features // 2
+        np_ = nz // 2
         chunk = nz * CAP
-        piece = chunk // nt
+        pieces = nt // 2
+        piece = chunk // pieces
         dma = pltpu.SemaphoreType.DMA
         any_ = pl.BlockSpec(memory_space=pl.ANY)
         ig, ag = pl.pallas_call(
@@ -310,19 +415,22 @@
                 pltpu.VMEM((count, features), BF16),
                 pltpu.VMEM((count, features), BF16),
                 pltpu.VMEM((features, hidden), BF16),
-                pltpu.VMEM((2, games, 16, half), BF16),
+                pltpu.VMEM((games, 2, 16, half), BF16),
+                pltpu.VMEM((ny, np_ // 2, 2, 16, half), BF16),
                 pltpu.VMEM((ny, nz, 16, half), BF16),
                 pltpu.VMEM((ny, chunk, features), BF16),
-                pltpu.VMEM((ny, nt, piece, hidden), part_type),
+                pltpu.VMEM((ny, pieces, piece, hidden), part_type),
                 pltpu.VMEM((ny, nt - 1, piece, hidden), part_type),
                 pltpu.VMEM((ny, piece, hidden), BF16),
                 pltpu.VMEM((ny, piece, hidden), BF16),
-                pltpu.VMEM((ny, nt, piece, hidden), BF16),
+                pltpu.VMEM((piece, hidden), F32),
+                pltpu.VMEM((ny, pieces, piece, hidden), BF16),
                 pltpu.VMEM((ny, nz, 16, half), BF16),
                 pltpu.VMEM((games, 16, half), BF16),
                 pltpu.VMEM((count, features), BF16),
                 pltpu.VMEM((features, hidden), BF16),
                 dma((3,)), dma((2,)), dma((2,)),
+                dma, dma((ny,)),
                 dma, dma((ny,)),
                 dma, dma((ny,)),
                 dma, dma((ny,)),

time: 134 us -> 113 us (0.84)
  Pallas kernels: 127 us -> 106 us
    pallas_call x1, Pallas kernels: 127 us -> 106 us  [body(): pl.pallas_call(functools.partial(kernel, ny, nz, nt, part_type), out_shap...]
where the time goes in v2:
time: 113 us
  Pallas kernels  106 us (94%)
  local copies, waits for them, and re-layouts  6.16 us (5%)
    pallas_call x1, Pallas kernels, body(): pl.pallas_call(functools.partial(kernel, ny, nz, nt, part_type), out_shap...  106 us
    unnamed x10, local copies, waits for them, and re-layouts  6.16 us

profile of v2, /device:TPU:1, one launch (start us, length us, event | category | flops | bytes accessed | tf_op | source)
XLA Modules:
  0.0 112.6 jit_solution(16010723998697718233)
XLA Ops:
  0.6 0.0 copy-start
  0.6 1.6 %copy-done = bf16[1,1024,1024]{2,1,0:T(8,128)(2,1)S(1)} copy-done((bf16[1,1024,1024]{2,1,0:T(8,128)(2,1)S(1)}, bf16[1,1024,1024]{2,1,0:T(8,128)(2,1)}, u32[]{:S(2)}) %copy-start) | copy-done | bytes 2097176
  2.2 0.0 copy-start.1
  2.2 0.9 copy-done.1
  3.2 0.0 copy-start.2
  3.2 0.9 copy-done.2
  4.1 0.0 copy-start.3
  4.1 0.7 copy-done.3
  4.8 105.8 %shard_map.59 = (bf16[128,1024]{1,0:T(8,128)(2,1)S(1)}, bf16[1024,1024]{1,0:T(8,128)(2,1)S(1)}) custom-call(s32[1,128]{1,0:T(1,128)S(1)} %bitcast.5, bf16[128,1024]{1,0:T(8,128)(2,1)S(1)} %copy-done.1, bf16[128,1024]{1,0:T(8,128)(2,1)S(1)} %copy-done.2, bf16[1024,1024]{1,0:T(8,128)(2,1)S(1)} %bitcast.3), custom_call_target="tpu_custom_call" | custom-call | tf_op jit(solution)/shard_map/pallas_call | solution.py:406
  110.6 0.7 copy.8
  111.3 1.3 %copy.9 = bf16[1,1024,1024]{2,1,0:T(8,128)(2,1)} copy(bf16[1,1024,1024]{2,1,0:T(8,128)(2,1)S(1)} %bitcast.4) | data formatting | bytes 4194304
Async XLA Ops:
  0.6 1.6 %copy-start = (bf16[1,1024,1024]{2,1,0:T(8,128)(2,1)S(1)}, bf16[1,1024,1024]{2,1,0:T(8,128)(2,1)}, u32[]{:S(2)}) copy-start(bf16[1,1024,1024]{2,1,0:T(8,128)(2,1)} %param.7) | copy-start | bytes 6291460
  2.2 0.9 copy-start.1
  3.2 0.9 copy-start.2
  4.1 0.7 copy-start.3

commit v3 on v2

--- a/solution.py
+++ b/solution.py
@@ -34,8 +34,8 @@
     ny, nz, nt, part_type,
     ids_ref, tok_hbm, cot_hbm, w_hbm,
     ig_hbm, ag_hbm,
-    tok, cot, w, sends, relay, arrived, rows, part, summands, swap_out, swap_in, slope, mixed, bsend, back, ig, ag,
-    in_sem, out_sem, self_sem, relay_send, relay_recv, fwd_send, fwd_recv, rs_send, rs_recv, swap_send, swap_recv, ag_send, ag_recv,
+    tok, cot, w, sends, relay, arrived, rows, pair_out, pair_in, own, part, summands, swap_out, swap_in, slope, mixed, bsend, back, ig, ag,
+    in_sem, out_sem, self_sem, relay_send, relay_recv, fwd_send, fwd_recv, pair_send, pair_recv, rs_send, rs_recv, pass_send, swap_send, swap_recv, ag_send, ag_recv,
     back_send, back_recv,
 ):
     nb = ny * nz
@@ -191,27 +191,41 @@
         rows[c, :, :half] = wide[:, 0].reshape(chunk, half).astype(BF16)
         rows[c, :, half:] = wide[:, 1].reshape(chunk, half).astype(BF16)
 
-        product = jnp.dot(rows[c], w[...], preferred_element_type=F32)
-        part[c] = product.reshape(pieces, piece, hidden).astype(part_type)
-
-        def send_part(k, _):
-            to = (x + k) % pieces
-
-            @pl.when(2 * to + gather_core != t)
-            def _send():
-                far = 2 * to + gather_core
+        product = jnp.dot(rows[c], w[...], preferred_element_type=F32).reshape(pieces, piece, hidden)
+
+        @pl.when(jnp.logical_not(gathers))
+        def _give():
+            pair_out[c] = product
+            pltpu.make_async_remote_copy(
+                src_ref=pair_out.at[c],
+                dst_ref=pair_in.at[c],
+                send_sem=pair_send,
+                recv_sem=pair_recv.at[c],
+                device_id={"tensor": sibling},
+                device_id_type=MESH,
+            ).start()
+
+        @pl.when(gathers)
+        def _take():
+            pair_out[c] = product
+            ref = pair_in.at[c]
+            pltpu.make_async_copy(ref, ref, pair_recv.at[c]).wait()
+            part[c] = (pair_out[c] + pair_in[c]).astype(part_type)
+            own[...] = pair_out[c, x] + pair_in[c, x]
+
+            def send_part(k, _):
+                to = (x + k) % pieces
                 pltpu.make_async_remote_copy(
                     src_ref=part.at[c, to],
-                    dst_ref=summands.at[c, (t - far + nt) % nt - 1],
+                    dst_ref=summands.at[c, pieces - k - 1],
                     send_sem=rs_send,
                     recv_sem=rs_recv.at[c],
-                    device_id={"tensor": far},
+                    device_id={"tensor": 2 * to + gather_core},
                     device_id_type=MESH,
                 ).start()
-
-            return _
-
-        lax.fori_loop(0, pieces, send_part, 0)
+                return _
+
+            lax.fori_loop(1, pieces, send_part, 0)
 
     def swap_copy(c):
         return pltpu.make_async_remote_copy(
@@ -224,11 +238,12 @@
         )
 
     def combine(c):
-        ref = summands.at[c]
-        pltpu.make_async_copy(ref, ref, rs_recv.at[c]).wait()
-        total = part[c, x].astype(F32)
-        for k in range(nt - 1):
-            total = total + summands[c, k].astype(F32)
+        total = own[...]
+        if pieces > 1:
+            ref = summands.at[c]
+            pltpu.make_async_copy(ref, ref, rs_recv.at[c]).wait()
+            for k in range(pieces - 1):
+                total = total + summands[c, k].astype(F32)
         swap_out[c] = jnp.where(par == 0, smooth_gate(total), total).astype(BF16)
         swap_copy(c).start()
         slope[...] = jnp.where(par == 0, gate_slope(total), 1.0)
@@ -243,21 +258,32 @@
                 dst_ref=mixed.at[c, x],
                 send_sem=ag_send,
                 recv_sem=ag_recv.at[c],
-                device_id={"tensor": (t + k) % nt},
+                device_id={"tensor": 2 * ((x + k) % pieces) + gather_core},
                 device_id_type=MESH,
             ).start()
             return _
 
-        lax.fori_loop(1, nt, send_mixed, 0)
+        lax.fori_loop(1, pieces, send_mixed, 0)
 
     def give_back(c):
-        for number, yes in ((pieces - 1, gathers), (pieces, jnp.logical_not(gathers))):
-            if number > 0:
-
-                @pl.when(yes)
-                def _wait():
-                    ref = mixed.at[c, pl.ds(0, number)]
-                    pltpu.make_async_copy(ref, ref, ag_recv.at[c]).wait()
+        @pl.when(gathers)
+        def _pass_on():
+            if pieces > 1:
+                ref = mixed.at[c, pl.ds(0, pieces - 1)]
+                pltpu.make_async_copy(ref, ref, ag_recv.at[c]).wait()
+            pltpu.make_async_remote_copy(
+                src_ref=mixed.at[c],
+                dst_ref=mixed.at[c],
+                send_sem=pass_send,
+                recv_sem=ag_recv.at[c],
+                device_id={"tensor": sibling},
+                device_id_type=MESH,
+            ).start()
+
+        @pl.when(jnp.logical_not(gathers))
+        def _passed():
+            ref = mixed.at[c]
+            pltpu.make_async_copy(ref, ref, ag_recv.at[c]).wait()
 
         @pl.when(par == 0)
         def _input_gradient():
@@ -373,11 +399,11 @@
             ref = mixed.at[:, pl.ds(0, pieces - 1)]
             pltpu.make_async_copy(ref, ref, ag_send).wait()
         pltpu.make_async_copy(swap_out, swap_out, swap_send).wait()
-        pltpu.make_async_copy(mixed, mixed, ag_send).wait()
+        pltpu.make_async_copy(mixed, mixed, pass_send).wait()
 
     @pl.when(jnp.logical_not(gathers))
     def _given():
-        pltpu.make_async_copy(part, part, rs_send).wait()
+        pltpu.make_async_copy(pair_out, pair_out, pair_send).wait()
 
     @pl.when(par == 0)
     def _sent_back():
@@ -419,8 +445,11 @@
                 pltpu.VMEM((ny, np_ // 2, 2, 16, half), BF16),
                 pltpu.VMEM((ny, nz, 16, half), BF16),
                 pltpu.VMEM((ny, chunk, features), BF16),
+                pltpu.VMEM((ny, pieces, piece, hidden), F32),
+                pltpu.VMEM((ny, pieces, piece, hidden), F32),
+                pltpu.VMEM((piece, hidden), F32),
                 pltpu.VMEM((ny, pieces, piece, hidden), part_type),
-                pltpu.VMEM((ny, nt - 1, piece, hidden), part_type),
+                pltpu.VMEM((ny, max(pieces - 1, 1), piece, hidden), part_type),
                 pltpu.VMEM((ny, piece, hidden), BF16),
                 pltpu.VMEM((ny, piece, hidden), BF16),
                 pltpu.VMEM((piece, hidden), F32),
@@ -434,6 +463,8 @@
                 dma, dma((ny,)),
                 dma, dma((ny,)),
                 dma, dma((ny,)),
+                dma,
+                dma, dma((ny,)),
                 dma, dma((ny,)),
                 dma, dma,
             ],

time: 113 us -> 109 us (0.965)
  the two profiles are of different devices: /device:TPU:1 before, /device:TPU:8 now
where the time goes in v3:
time: 109 us
  Pallas kernels  102 us (94%)
  local copies, waits for them, and re-layouts  6.16 us (6%)
    pallas_call x1, Pallas kernels, body(): pl.pallas_call(functools.partial(kernel, ny, nz, nt, part_type), out_shap...  102 us
    unnamed x10, local copies, waits for them, and re-layouts  6.16 us

profile of v3, /device:TPU:8, one launch (start us, length us, event | category | flops | bytes accessed | tf_op | source)
XLA Modules:
  0.0 108.6 jit_solution(14905071482629898043)
XLA Ops:
  0.6 0.0 copy-start
  0.6 1.6 %copy-done = bf16[1,1024,1024]{2,1,0:T(8,128)(2,1)S(1)} copy-done((bf16[1,1024,1024]{2,1,0:T(8,128)(2,1)S(1)}, bf16[1,1024,1024]{2,1,0:T(8,128)(2,1)}, u32[]{:S(2)}) %copy-start) | copy-done | bytes 2097176
  2.2 0.0 copy-start.1
  2.2 0.9 copy-done.1
  3.2 0.0 copy-start.2
  3.2 0.9 copy-done.2
  4.1 0.0 copy-start.3
  4.1 0.7 copy-done.3
  4.8 101.8 %shard_map.59 = (bf16[128,1024]{1,0:T(8,128)(2,1)S(1)}, bf16[1024,1024]{1,0:T(8,128)(2,1)S(1)}) custom-call(s32[1,128]{1,0:T(1,128)S(1)} %bitcast.5, bf16[128,1024]{1,0:T(8,128)(2,1)S(1)} %copy-done.1, bf16[128,1024]{1,0:T(8,128)(2,1)S(1)} %copy-done.2, bf16[1024,1024]{1,0:T(8,128)(2,1)S(1)} %bitcast.3), custom_call_target="tpu_custom_call" | custom-call | tf_op jit(solution)/shard_map/pallas_call | solution.py:432
  106.6 0.7 copy.8
  107.3 1.3 %copy.9 = bf16[1,1024,1024]{2,1,0:T(8,128)(2,1)} copy(bf16[1,1024,1024]{2,1,0:T(8,128)(2,1)S(1)} %bitcast.4) | data formatting | bytes 4194304
Async XLA Ops:
  0.6 1.6 %copy-start = (bf16[1,1024,1024]{2,1,0:T(8,128)(2,1)S(1)}, bf16[1,1024,1024]{2,1,0:T(8,128)(2,1)}, u32[]{:S(2)}) copy-start(bf16[1,1024,1024]{2,1,0:T(8,128)(2,1)} %param.7) | copy-start | bytes 6291460
  2.2 0.9 copy-start.1
  3.2 0.9 copy-start.2
  4.1 0.7 copy-start.3

commit v4 on v3

--- a/solution.py
+++ b/solution.py
@@ -183,35 +183,34 @@
             ref = arrived.at[c]
             pltpu.make_async_copy(ref, ref, fwd_recv.at[c]).wait()
 
-        @pl.when(c + AHEAD < ny)
-        def _next():
-            send_forward(c + AHEAD, 0)
-
         wide = arrived[c].astype(F32).reshape(nz, 2, CAP, half)
         rows[c, :, :half] = wide[:, 0].reshape(chunk, half).astype(BF16)
         rows[c, :, half:] = wide[:, 1].reshape(chunk, half).astype(BF16)
 
-        product = jnp.dot(rows[c], w[...], preferred_element_type=F32).reshape(pieces, piece, hidden)
-
-        @pl.when(jnp.logical_not(gathers))
-        def _give():
-            pair_out[c] = product
-            pltpu.make_async_remote_copy(
-                src_ref=pair_out.at[c],
-                dst_ref=pair_in.at[c],
-                send_sem=pair_send,
-                recv_sem=pair_recv.at[c],
-                device_id={"tensor": sibling},
-                device_id_type=MESH,
-            ).start()
+        for h in range(2):
+            cols = slice(h * (hidden // 2), (h + 1) * (hidden // 2))
+            product = jnp.dot(rows[c], w[:, cols], preferred_element_type=F32)
+            pair_out[c, h] = product.reshape(pieces, piece, hidden // 2)
+
+            @pl.when(jnp.logical_not(gathers))
+            def _give():
+                pltpu.make_async_remote_copy(
+                    src_ref=pair_out.at[c, h],
+                    dst_ref=pair_in.at[c, h],
+                    send_sem=pair_send,
+                    recv_sem=pair_recv.at[c, h],
+                    device_id={"tensor": sibling},
+                    device_id_type=MESH,
+                ).start()
 
         @pl.when(gathers)
         def _take():
-            pair_out[c] = product
-            ref = pair_in.at[c]
-            pltpu.make_async_copy(ref, ref, pair_recv.at[c]).wait()
-            part[c] = (pair_out[c] + pair_in[c]).astype(part_type)
-            own[...] = pair_out[c, x] + pair_in[c, x]
+            for h in range(2):
+                cols = slice(h * (hidden // 2), (h + 1) * (hidden // 2))
+                ref = pair_in.at[c, h]
+                pltpu.make_async_copy(ref, ref, pair_recv.at[c, h]).wait()
+                part[c, :, :, cols] = (pair_out[c, h] + pair_in[c, h]).astype(part_type)
+                own[:, cols] = pair_out[c, h, x] + pair_in[c, h, x]
 
             def send_part(k, _):
                 to = (x + k) % pieces
@@ -226,6 +225,10 @@
                 return _
 
             lax.fori_loop(1, pieces, send_part, 0)
+
+        @pl.when(c + AHEAD < ny)
+        def _next():
+            send_forward(c + AHEAD, 0)
 
     def swap_copy(c):
         return pltpu.make_async_remote_copy(
@@ -285,6 +288,7 @@
             ref = mixed.at[c]
             pltpu.make_async_copy(ref, ref, ag_recv.at[c]).wait()
 
+    def gradient(c):
         @pl.when(par == 0)
         def _input_gradient():
             grad = lax.dot_general(
@@ -336,6 +340,7 @@
 
         @pl.when(k > 0)
         def _start_back():
+            gradient(k - 1)
             start_back(k - 1)
 
         @pl.when((k < ny) & gathers)
@@ -445,8 +450,8 @@
                 pltpu.VMEM((ny, np_ // 2, 2, 16, half), BF16),
                 pltpu.VMEM((ny, nz, 16, half), BF16),
                 pltpu.VMEM((ny, chunk, features), BF16),
-                pltpu.VMEM((ny, pieces, piece, hidden), F32),
-                pltpu.VMEM((ny, pieces, piece, hidden), F32),
+                pltpu.VMEM((ny, 2, pieces, piece, hidden // 2), F32),
+                pltpu.VMEM((ny, 2, pieces, piece, hidden // 2), F32),
                 pltpu.VMEM((piece, hidden), F32),
                 pltpu.VMEM((ny, pieces, piece, hidden), part_type),
                 pltpu.VMEM((ny, max(pieces - 1, 1), piece, hidden), part_type),
@@ -461,7 +466,7 @@
                 dma((3,)), dma((2,)), dma((2,)),
                 dma, dma((ny,)),
                 dma, dma((ny,)),
-                dma, dma((ny,)),
+                dma, dma((ny, 2)),
                 dma, dma((ny,)),
                 dma,
                 dma, dma((ny,)),

time: 109 us -> 108 us (level)
  the two profiles are of different devices: /device:TPU:8 before, /device:TPU:1 now
where the time goes in v4:
time: 108 us; the launch traced here: 107 us
  Pallas kernels  99.7 us (92%)
  local copies, waits for them, and re-layouts  6.16 us (6%)
    pallas_call x1, Pallas kernels, body(): pl.pallas_call(functools.partial(kernel, ny, nz, nt, part_type), out_shap...  99.7 us
    unnamed x10, local copies, waits for them, and re-layouts  6.16 us

profile of v4, /device:TPU:1, one launch (start us, length us, event | category | flops | bytes accessed | tf_op | source)
XLA Modules:
  0.0 106.6 jit_solution(558588874640679753)
XLA Ops:
  0.6 0.0 copy-start
  0.6 1.6 %copy-done = bf16[1,1024,1024]{2,1,0:T(8,128)(2,1)S(1)} copy-done((bf16[1,1024,1024]{2,1,0:T(8,128)(2,1)S(1)}, bf16[1,1024,1024]{2,1,0:T(8,128)(2,1)}, u32[]{:S(2)}) %copy-start) | copy-done | bytes 2097176
  2.2 0.0 copy-start.1
  2.2 0.9 copy-done.1
  3.2 0.0 copy-start.2
  3.2 0.9 copy-done.2
  4.1 0.0 copy-start.3
  4.1 0.7 copy-done.3
  4.8 99.7 %shard_map.59 = (bf16[128,1024]{1,0:T(8,128)(2,1)S(1)}, bf16[1024,1024]{1,0:T(8,128)(2,1)S(1)}) custom-call(s32[1,128]{1,0:T(1,128)S(1)} %bitcast.5, bf16[128,1024]{1,0:T(8,128)(2,1)S(1)} %copy-done.1, bf16[128,1024]{1,0:T(8,128)(2,1)S(1)} %copy-done.2, bf16[1024,1024]{1,0:T(8,128)(2,1)S(1)} %bitcast.3), custom_call_target="tpu_custom_call" | custom-call | tf_op jit(solution)/shard_map/pallas_call | solution.py:437
  104.5 0.7 copy.8
  105.2 1.3 %copy.9 = bf16[1,1024,1024]{2,1,0:T(8,128)(2,1)} copy(bf16[1,1024,1024]{2,1,0:T(8,128)(2,1)S(1)} %bitcast.4) | data formatting | bytes 4194304
Async XLA Ops:
  0.6 1.6 %copy-start = (bf16[1,1024,1024]{2,1,0:T(8,128)(2,1)S(1)}, bf16[1,1024,1024]{2,1,0:T(8,128)(2,1)}, u32[]{:S(2)}) copy-start(bf16[1,1024,1024]{2,1,0:T(8,128)(2,1)} %param.7) | copy-start | bytes 6291460
  2.2 0.9 copy-start.1
  3.2 0.9 copy-start.2
  4.1 0.7 copy-start.3
